TPU v7x, 32 devices: a whole 2x2x4 slice. The times are simulated.
32 devices in a mesh: ord: 16 (over z, y, x), rhs: 2 (over core).
Axes of the slice: x: 2, y: 2, z: 4, core: 2. Of those that a mesh axis runs over, the one named last changes fastest.
Arguments:
- rhs_blocks: float32 [128, 640, 128], P('ord', None, 'rhs'), may hold values from -6 to 6
- rhs_border: float32 [512, 128], P(None, 'rhs'), may hold values from -6 to 6
- start_blocks: float32 [128, 640, 128], P('ord', None, 'rhs'), may hold values from -3 to 3
- start_border: float32 [512, 128], P(None, 'rhs'), may hold values from -3 to 3
- diag_blocks: bfloat16 [128, 640, 640], P('ord'), may hold values from -1 to 9
- block_inverses: bfloat16 [128, 640, 640], P('ord'), may hold values from -6 to 6
- couplings: bfloat16 [128, 640, 640], P('ord'), may hold values from -0.125 to 0.125
- border_couplings: bfloat16 [128, 640, 512], P('ord'), may hold values from -0.01953125 to 0.01953125
- border_block: bfloat16 [512, 512], replicated, may hold values from -1 to 9
- schur_inverse: float32 [512, 512], replicated, may hold values from -6 to 6
- row_counts: int32 [128], P('ord'), may hold values from 1 to 640, as said below
Outputs:
- solution_blocks: float32 [128, 640, 128], P('ord', None, 'rhs')
- solution_border: float32 [512, 128], P(None, 'rhs')
Inputs may be any that keep to these rules, and one draw needn't show every extreme that they name: row_counts[m] is the number of live rows of order block m; block 0 has exactly 640 rows and the counts fall with the order to about a third of 640.
All inputs are finite; a program needn't handle non-finite values.
Results may differ from a plain program's by a relative error of at most 0.0035.
Values may be sent and summed in bfloat16 or wider, within the bound.
A program may use at most 128 MiB of HBM per device.

v0:
```python
import jax
import jax.numpy as jnp
from jax import lax
from jax.sharding import PartitionSpec as P

ITERS = 3


def shifted(value, axis, steps):
    count = lax.axis_size(axis)
    leading, last = (max(0, -steps), min(count, count - steps))
    return lax.ppermute(value, axis, [(source, source + steps) for source in range(leading, last)])


def batched(matrices, vectors):
    return jnp.einsum("sij,sjc->sic", matrices, vectors, preferred_element_type=jnp.float32)


def shards(
    rhs_blocks,
    rhs_border,
    start_blocks,
    start_border,
    diag_blocks,
    block_inverses,
    couplings,
    border_couplings,
    border_block,
    schur_inverse,
    row_counts,
):
    slot_count = rhs_blocks.shape[0]
    row_total = rhs_blocks.shape[1]
    live_rows = (
        lax.broadcasted_iota(jnp.int32, (slot_count, row_total), 1) < row_counts[:, None]
    ).astype(jnp.float32)[:, :, None]

    def operate(state, state_border, against):
        narrow = state.astype(jnp.bfloat16)
        narrow_border = state_border.astype(jnp.bfloat16)
        upper = shifted(narrow[:1], "ord", -1)
        ahead = batched(couplings, jnp.concatenate([narrow[1:], upper], 0))
        transposed = jnp.einsum(
            "sji,sjc->sic", couplings, narrow, preferred_element_type=jnp.float32
        )
        lower = shifted(transposed[slot_count - 1 :].astype(jnp.bfloat16), "ord", 1).astype(
            jnp.float32
        )
        behind = jnp.concatenate([lower, transposed[:-1]], 0)
        from_border = jnp.einsum(
            "sib,bc->sic", border_couplings, narrow_border, preferred_element_type=jnp.float32
        )
        applied = live_rows * (batched(diag_blocks, narrow) + ahead + behind + from_border)
        gathered = jnp.einsum(
            "sib,sic->bc", border_couplings, narrow, preferred_element_type=jnp.float32
        )
        block_numerator = jnp.sum(against * applied)
        block_denominator = jnp.sum(applied * applied)
        gathered, block_numerator, block_denominator = lax.psum(
            (gathered, block_numerator, block_denominator), "ord"
        )
        applied_border = (
            jnp.dot(border_block, narrow_border, preferred_element_type=jnp.float32) + gathered
        )
        return (applied, applied_border, block_numerator, block_denominator)

    solution = live_rows * start_blocks
    solution_border = start_border
    applied, applied_border, unused_num, unused_den = operate(
        solution, solution_border, jnp.zeros_like(solution)
    )
    residual = live_rows * rhs_blocks - applied
    resid_border = rhs_border - applied_border
    for iteration in range(ITERS):
        blockwise = live_rows * batched(block_inverses, residual.astype(jnp.bfloat16))
        border_sum = jnp.einsum(
            "sib,sic->bc",
            border_couplings,
            blockwise.astype(jnp.bfloat16),
            preferred_element_type=jnp.float32,
        )
        total_sum = lax.psum(border_sum, "ord")
        update_border = jnp.dot(
            schur_inverse, resid_border - total_sum, precision=lax.Precision.HIGHEST
        )
        lifted = jnp.einsum(
            "sib,bc->sic",
            border_couplings,
            update_border.astype(jnp.bfloat16),
            preferred_element_type=jnp.float32,
        ).astype(jnp.bfloat16)
        update = blockwise - live_rows * batched(block_inverses, lifted)
        update, update_border = (update, update_border)
        applied, applied_border, block_numerator, block_denominator = operate(
            update, update_border, residual
        )
        border_numerator = jnp.sum(resid_border * applied_border)
        border_denominator = jnp.sum(applied_border * applied_border)
        numerator, denominator = lax.psum(
            (block_numerator + border_numerator, block_denominator + border_denominator), "rhs"
        )
        step_size = numerator / (denominator + 1e-06)
        solution = solution + step_size * update
        solution_border = solution_border + step_size * update_border
        residual = residual - step_size * applied
        resid_border = resid_border - step_size * applied_border
    return (solution, solution_border)


def solution(mesh):
    return jax.shard_map(
        shards,
        mesh=mesh,
        in_specs=(
            P("ord", None, "rhs"),
            P(None, "rhs"),
            P("ord", None, "rhs"),
            P(None, "rhs"),
            P("ord", None, None),
            P("ord", None, None),
            P("ord", None, None),
            P("ord", None, None),
            P(),
            P(),
            P("ord"),
        ),
        out_specs=(P("ord", None, "rhs"), P(None, "rhs")),
        check_vma=False,
    )
```

profile of v0, /device:TPU:0, one launch (start us, length us, event | category | flops | bytes accessed | tf_op | source)
XLA Modules:
  0.0 814.8 jit_solution(3633228411959776804)
XLA Ops:
  11.2 4.7 convolution_bitcast_fusion.6
  15.9 5.0 collective-permute-start.1
  35.4 109.5 %all-reduce.24.cloned.1.call-done = (f32[512,64]{0,1:T(8,128)}, f32[512,64]{0,1:T(8,128)}) async-done(((f32[512,64]{0,1:T(8,128)}, f32[512,64]{0,1:T(8,128)}), (f32[512,64]{0,1:T(8,128)}, f32[512,64]{0,1:T(8,128)})) %all-reduce.24.cloned.1.call-update) | async-done | bytes 262160 | tf_op jit(solution)/shard_map/psum | solution.py:59
  148.6 4.3 convolution_bitcast_fusion.5
  153.0 3.3 fusion.75
  158.4 3.3 fusion.79
  163.6 4.6 collective-permute-start.3
  173.6 7.9 multiply_reduce_fusion.4
  181.5 39.8 %all-reduce.2 = (f32[]{:T(128)}, f32[]{:T(128)}) all-reduce(f32[]{:T(128)} %get-tuple-element.7, f32[]{:T(128)} %get-tuple-element.6), channel_id=1, replica_groups=mesh['ord'=16,'rhs'=2] {'ord'}, use_global_device_ids=true, to_apply=%region_3.0 | all-reduce | flops 2 | bytes 16 | tf_op jit(solution)/shard_map/psum | solution.py:59
  221.3 57.3 %all-reduce.14.cloned.1.call-done = f32[512,64]{0,1:T(8,128)} async-done(((f32[512,64]{0,1:T(8,128)}), f32[512,64]{0,1:T(8,128)}) %all-reduce.14.cloned.1.call-update) | async-done | bytes 131088 | tf_op jit(solution)/shard_map/psum | solution.py:59
  283.2 3.0 all-reduce.6
  289.4 5.6 convolution_multiply_fusion.3
  298.0 103.0 %all-reduce.16.cloned.1.call-done = f32[512,64]{0,1:T(8,128)} async-done(((f32[512,64]{0,1:T(8,128)}), f32[512,64]{0,1:T(8,128)}) %all-reduce.16.cloned.1.call-update) | async-done | bytes 131088 | tf_op jit(solution)/shard_map/psum | solution.py:82
  403.8 4.3 convolution_bitcast_fusion.3
  408.1 6.7 fusion.76
  416.5 3.3 fusion.80
  422.4 5.2 collective-permute-start.5
  433.6 8.1 multiply_reduce_fusion.2
  441.7 39.5 %all-reduce.1 = (f32[]{:T(128)}, f32[]{:T(128)}) all-reduce(f32[]{:T(128)} %get-tuple-element.5, f32[]{:T(128)} %get-tuple-element.4), channel_id=1, replica_groups=mesh['ord'=16,'rhs'=2] {'ord'}, use_global_device_ids=true, to_apply=%region_13.0 | all-reduce | flops 2 | bytes 16 | tf_op jit(solution)/shard_map/psum | solution.py:59
  481.2 55.9 %all-reduce.18.cloned.1.call-done = f32[512,64]{0,1:T(8,128)} async-done(((f32[512,64]{0,1:T(8,128)}), f32[512,64]{0,1:T(8,128)}) %all-reduce.18.cloned.1.call-update) | async-done | bytes 131088 | tf_op jit(solution)/shard_map/psum | solution.py:59
  542.2 3.0 all-reduce.5
  546.6 5.5 convolution_multiply_fusion.1
  553.2 4.3 convolution_bitcast_fusion.11
  557.8 103.1 %all-reduce.20.cloned.1.call-done = f32[512,64]{0,1:T(8,128)} async-done(((f32[512,64]{0,1:T(8,128)}), f32[512,64]{0,1:T(8,128)}) %all-reduce.20.cloned.1.call-update) | async-done | bytes 131088 | tf_op jit(solution)/shard_map/psum | solution.py:82
  663.2 4.3 convolution_bitcast_fusion.1
  667.7 3.3 fusion.77
  673.1 3.4 fusion.81
  678.4 4.5 collective-permute-start.7
  689.1 7.4 multiply_reduce_fusion
  696.5 39.5 %all-reduce = (f32[]{:T(128)}, f32[]{:T(128)}) all-reduce(f32[]{:T(128)} %get-tuple-element.3, f32[]{:T(128)} %get-tuple-element.2), channel_id=1, replica_groups=mesh['ord'=16,'rhs'=2] {'ord'}, use_global_device_ids=true, to_apply=%region_23.0 | all-reduce | flops 2 | bytes 16 | tf_op jit(solution)/shard_map/psum | solution.py:59
  736.1 58.1 %all-reduce.22.cloned.1.call-done = f32[512,64]{0,1:T(8,128)} async-done(((f32[512,64]{0,1:T(8,128)}), f32[512,64]{0,1:T(8,128)}) %all-reduce.22.cloned.1.call-update) | async-done | bytes 131088 | tf_op jit(solution)/shard_map/psum | solution.py:59
  804.5 3.5 bitcast_add_fusion
  (232 shorter events, 74.0 us)
Async XLA Ops:
  7.2 139.2 %copy-start = (f32[512,512]{1,0:T(8,128)S(1)}, f32[512,512]{1,0:T(8,128)}, u32[]{:S(2)}) copy-start(f32[512,512]{1,0:T(8,128)} %param.20) | copy-start | bytes 3145732
  7.2 137.7 %all-reduce.24.cloned.1.call-start = ((), (), s32[]{:S(2)}) async-start(), calls=%async_computation.5 | async-start | bytes 524288 | tf_op jit(solution)/shard_map/psum | solution.py:59
  8.0 144.9 %copy-start.22 = (f32[8,640]{1,0:T(8,128)}, f32[8,640]{1,0:T(8,128)S(1)}, u32[]{:S(2)}) copy-start(f32[8,640]{1,0:T(8,128)S(1)} %fusion.67) | copy-start | bytes 61444
  9.7 17.1 %collective-permute-start = (bf16[1,640,64]{1,2,0:T(8,128)(2,1)S(1)}, bf16[1,640,64]{1,2,0:T(8,128)(2,1)S(1)}, u32[]{:S(2)}, u32[]{:S(2)}) collective-permute-start(bf16[1,640,64]{1,2,0:T(8,128)(2,1)S(1)} %slice.69), channel_id=1, source_target_pairs={{2,0},{4,2},{6,4},{8,6},{10,8},{12,10},{14,12},{16,14},{18,16},{20... | collective-permute-start | bytes 245768 | tf_op jit(solution)/shard_map/ppermute | solution.py:12
  15.9 10.8 %collective-permute-start.1 = (bf16[1,640,64]{1,2,0:T(8,128)(2,1)S(1)}, bf16[1,640,64]{1,2,0:T(8,128)(2,1)S(1)}, u32[]{:S(2)}, u32[]{:S(2)}) collective-permute-start(bf16[1,640,64]{1,2,0:T(8,128)(2,1)S(1)} %slice.91), channel_id=1, source_target_pairs={{0,2},{2,4},{4,6},{6,8},{8,10},{10,12},{12,14},{14,16},{16,18},{18... | collective-permute-start | bytes 245768 | tf_op jit(solution)/shard_map/ppermute | solution.py:12
  33.5 119.4 %slice-start.20 = ((s8[6553600]{0:T(1024)(128)(4,1)}), s8[2359296]{0:T(1024)(128)(4,1)S(1)}, s32[]{:S(2)}) async-start(s8[6553600]{0:T(1024)(128)(4,1)} %bitcast.203), calls=%async_computation.26 | async-start | bytes 4718592
  35.2 243.5 %all-reduce.14.cloned.1.call-start = ((), (), s32[]{:S(2)}) async-start(), calls=%async_computation | async-start | bytes 262144 | tf_op jit(solution)/shard_map/psum | solution.py:59
  153.0 15.2 %slice-start.2 = ((s8[5242880]{0:T(1024)(128)(4,1)}), s8[1048576]{0:T(1024)(128)(4,1)S(1)}, s32[]{:S(2)}) async-start(s8[5242880]{0:T(1024)(128)(4,1)} %bitcast.185), calls=%async_computation.8 | async-start | bytes 2097152
  162.3 11.3 %collective-permute-start.2 = (bf16[1,640,64]{1,2,0:T(8,128)(2,1)}, bf16[1,640,64]{1,2,0:T(8,128)(2,1)}, u32[]{:S(2)}, u32[]{:S(2)}) collective-permute-start(bf16[1,640,64]{1,2,0:T(8,128)(2,1)} %slice.73), channel_id=1, source_target_pairs={{2,0},{4,2},{6,4},{8,6},{10,8},{12,10},{14,12},{16,14},{18,16},{20... | collective-permute-start | bytes 245768 | tf_op jit(solution)/shard_map/ppermute | solution.py:12
  163.6 9.9 %collective-permute-start.3 = (bf16[1,640,64]{1,2,0:T(8,128)(2,1)S(1)}, bf16[1,640,64]{1,2,0:T(8,128)(2,1)S(1)}, u32[]{:S(2)}, u32[]{:S(2)}) collective-permute-start(bf16[1,640,64]{1,2,0:T(8,128)(2,1)S(1)} %slice.90), channel_id=1, source_target_pairs={{0,2},{2,4},{4,6},{6,8},{8,10},{10,12},{12,14},{14,16},{16,18},{18... | collective-permute-start | bytes 245768 | tf_op jit(solution)/shard_map/ppermute | solution.py:12
  173.5 227.6 %all-reduce.16.cloned.1.call-start = ((), (), s32[]{:S(2)}) async-start(), calls=%async_computation.1 | async-start | bytes 262144 | tf_op jit(solution)/shard_map/psum | solution.py:82
  173.6 105.1 %copy-start.16 = (bf16[512,512]{1,0:T(8,128)(2,1)S(1)}, bf16[512,512]{1,0:T(8,128)(2,1)}, u32[]{:S(2)}) copy-start(bf16[512,512]{1,0:T(8,128)(2,1)} %param.19) | copy-start | bytes 1572868
  289.4 257.2 %copy-start.1 = (f32[8,640,64]{1,2,0:T(8,128)}, f32[8,640,64]{1,2,0:T(8,128)S(1)}, u32[]{:S(2)}) copy-start(f32[8,640,64]{1,2,0:T(8,128)S(1)} %multiply_subtract_fusion.1) | copy-start | bytes 3932164
  297.7 239.4 %all-reduce.18.cloned.1.call-start = ((), (), s32[]{:S(2)}) async-start(), calls=%async_computation.2 | async-start | bytes 262144 | tf_op jit(solution)/shard_map/psum | solution.py:59
  298.0 105.1 %copy-start.27 = (f32[512,64]{0,1:T(8,128)}, f32[512,64]{0,1:T(8,128)S(1)}, u32[]{:S(2)}) copy-start(f32[512,64]{0,1:T(8,128)S(1)} %multiply_subtract_fusion.4) | copy-start | bytes 393220
  408.1 19.4 %slice-start.6 = ((s8[5242880]{0:T(1024)(128)(4,1)}), s8[1048576]{0:T(1024)(128)(4,1)S(1)}, s32[]{:S(2)}) async-start(s8[5242880]{0:T(1024)(128)(4,1)} %bitcast.189), calls=%async_computation.12 | async-start | bytes 2097152
  420.5 13.2 %collective-permute-start.4 = (bf16[1,640,64]{1,2,0:T(8,128)(2,1)}, bf16[1,640,64]{1,2,0:T(8,128)(2,1)}, u32[]{:S(2)}, u32[]{:S(2)}) collective-permute-start(bf16[1,640,64]{1,2,0:T(8,128)(2,1)} %slice.77), channel_id=1, source_target_pairs={{2,0},{4,2},{6,4},{8,6},{10,8},{12,10},{14,12},{16,14},{18,16},{20... | collective-permute-start | bytes 245768 | tf_op jit(solution)/shard_map/ppermute | solution.py:12
  422.4 10.3 %collective-permute-start.5 = (bf16[1,640,64]{1,2,0:T(8,128)(2,1)}, bf16[1,640,64]{1,2,0:T(8,128)(2,1)}, u32[]{:S(2)}, u32[]{:S(2)}) collective-permute-start(bf16[1,640,64]{1,2,0:T(8,128)(2,1)} %slice.89), channel_id=1, source_target_pairs={{0,2},{2,4},{4,6},{6,8},{8,10},{10,12},{12,14},{14,16},{16,18},{18... | collective-permute-start | bytes 245768 | tf_op jit(solution)/shard_map/ppermute | solution.py:12
  432.6 228.3 %all-reduce.20.cloned.1.call-start = ((), (), s32[]{:S(2)}) async-start(), calls=%async_computation.3 | async-start | bytes 262144 | tf_op jit(solution)/shard_map/psum | solution.py:82
  433.6 103.5 %copy-start.28 = (f32[512,64]{0,1:T(8,128)S(1)}, f32[512,64]{0,1:T(8,128)}, u32[]{:S(2)}) copy-start(f32[512,64]{0,1:T(8,128)} %copy-done.27) | copy-start | bytes 393220
  433.6 103.5 %copy-start.35 = (f32[64,512]{1,0:T(8,128)S(1)}, f32[64,512]{1,0:T(8,128)}, u32[]{:S(2)}) copy-start(f32[64,512]{1,0:T(8,128)} %copy-done.34) | copy-start | bytes 393220
  553.2 114.4 %slice-start.22 = ((s8[6553600]{0:T(1024)(128)(4,1)}), s8[2359296]{0:T(1024)(128)(4,1)S(1)}, s32[]{:S(2)}) async-start(s8[6553600]{0:T(1024)(128)(4,1)} %bitcast.205), calls=%async_computation.28 | async-start | bytes 4718592
  557.5 236.7 %all-reduce.22.cloned.1.call-start = ((), (), s32[]{:S(2)}) async-start(), calls=%async_computation.4 | async-start | bytes 262144 | tf_op jit(solution)/shard_map/psum | solution.py:59
  667.7 15.3 %slice-start.8 = ((s8[5242880]{0:T(1024)(128)(4,1)}), s8[1048576]{0:T(1024)(128)(4,1)S(1)}, s32[]{:S(2)}) async-start(s8[5242880]{0:T(1024)(128)(4,1)} %bitcast.191), calls=%async_computation.14 | async-start | bytes 2097152
  677.1 12.0 %collective-permute-start.6 = (bf16[1,640,64]{1,2,0:T(8,128)(2,1)}, bf16[1,640,64]{1,2,0:T(8,128)(2,1)S(1)}, u32[]{:S(2)}, u32[]{:S(2)}) collective-permute-start(bf16[1,640,64]{1,2,0:T(8,128)(2,1)} %slice.81), channel_id=1, source_target_pairs={{2,0},{4,2},{6,4},{8,6},{10,8},{12,10},{14,12},{16,14},{18,16},{20... | collective-permute-start | bytes 245768 | tf_op jit(solution)/shard_map/ppermute | solution.py:12
  678.4 10.6 %collective-permute-start.7 = (bf16[1,640,64]{1,2,0:T(8,128)(2,1)S(1)}, bf16[1,640,64]{1,2,0:T(8,128)(2,1)S(1)}, u32[]{:S(2)}, u32[]{:S(2)}) collective-permute-start(bf16[1,640,64]{1,2,0:T(8,128)(2,1)S(1)} %slice.88), channel_id=1, source_target_pairs={{0,2},{2,4},{4,6},{6,8},{8,10},{10,12},{12,14},{14,16},{16,18},{18... | collective-permute-start | bytes 245768 | tf_op jit(solution)/shard_map/ppermute | solution.py:12
  689.0 105.1 %copy-start.17 = (bf16[512,512]{1,0:T(8,128)(2,1)S(1)}, bf16[512,512]{1,0:T(8,128)(2,1)}, u32[]{:S(2)}) copy-start(bf16[512,512]{1,0:T(8,128)(2,1)} %param.19) | copy-start | bytes 1572868
  689.1 105.1 %copy-start.29 = (f32[512,64]{0,1:T(8,128)S(1)}, f32[512,64]{0,1:T(8,128)}, u32[]{:S(2)}) copy-start(f32[512,64]{0,1:T(8,128)} %copy-done.27) | copy-start | bytes 393220
  689.1 105.1 %copy-start.31 = (f32[64,512]{1,0:T(8,128)S(1)}, f32[64,512]{1,0:T(8,128)}, u32[]{:S(2)}) copy-start(f32[64,512]{1,0:T(8,128)} %copy-done.30) | copy-start | bytes 393220
  689.1 113.8 %copy-start.33 = (f32[64,512]{1,0:T(8,128)S(1)}, f32[64,512]{1,0:T(8,128)}, u32[]{:S(2)}) copy-start(f32[64,512]{1,0:T(8,128)} %copy-done.32) | copy-start | bytes 393220
  689.1 113.8 %copy-start.36 = (f32[64,512]{1,0:T(8,128)S(1)}, f32[64,512]{1,0:T(8,128)}, u32[]{:S(2)}) copy-start(f32[64,512]{1,0:T(8,128)} %copy-done.34) | copy-start | bytes 393220
  696.5 108.0 %copy-start.21 = (f32[8,64,640]{2,1,0:T(8,128)S(1)}, f32[8,64,640]{2,1,0:T(8,128)}, u32[]{:S(2)}) copy-start(f32[8,64,640]{2,1,0:T(8,128)} %get-tuple-element.29) | copy-start | bytes 3932164
  (55 other events, 310.9 us)
Sparse Core Ops, SparseCore 0:
  35.3 109.5 all-reduce.23
  173.6 104.9 all-reduce.13
  297.8 103.1 all-reduce.15
  432.7 104.3 all-reduce.17
  557.6 103.2 all-reduce.19
  689.1 105.0 all-reduce.21
where the time goes:
time: 816 us; the launch traced here: 815 us
  waiting for transfers between devices  487 us (60%)
  blocking collectives  128 us (16%)
  matrix products  116 us (14%)
  between operations  26.6 us (3%)
  starting transfers between devices  25.6 us (3%)
  local copies, waits for them, and re-layouts  21.4 us (3%)
  other arithmetic  10.4 us (1%)
    psum x4, waiting for transfers between devices, operate(): lax.psum((gathered, block_numerator, block_denominator), 'ord')  281 us
    psum x2, waiting for transfers between devices, shards(): total_sum = lax.psum(border_sum, 'ord')  206 us
    psum x3, blocking collectives, operate(): lax.psum((gathered, block_numerator, block_denominator), 'ord')  119 us
    dot_general x14, matrix products, batched(): jnp.einsum('sij,sjc->sic', matrices, vectors, preferred_element_type=jnp....  64.4 us
    ppermute x8, starting transfers between devices, shifted(): lax.ppermute(value, axis, [(source, source + steps) for source in range(l...  24.7 us
  transfers between devices with their start and end apart: 14, of which 6 were waited for; matrix products, arithmetic and copies ran while one was open for 6% of the time, Pallas kernels for 0%

commit v1 on v0

v1 whole, which is shorter than its diff:
```python
import functools

import jax
import jax.numpy as jnp
from jax import lax
from jax.experimental import pallas as pl
from jax.experimental.pallas import tpu as pltpu
from jax.sharding import PartitionSpec as P

ITERS = 3
MESH = pl.DeviceIdType.MESH
F32 = jnp.float32
BF16 = jnp.bfloat16


def mm(left, right):
    return jnp.dot(left, right, preferred_element_type=F32)


def kernel(
    count,
    rhs_hbm,
    start_hbm,
    diag_hbm,
    inverse_hbm,
    coupling_hbm,
    border_hbm,
    rhs_border_ref,
    start_border_ref,
    corner_ref,
    schur_ref,
    counts_ref,
    out_ref,
    out_border_ref,
    diag,
    inverse,
    coupling,
    coupling_t,
    border,
    border_t,
    rhs_own,
    rhs_land,
    start_own,
    start_land,
    rhs_border_land,
    start_border_land,
    sol,
    resid,
    update,
    applied,
    narrow,
    upper,
    lower_send,
    lower,
    resid_b,
    sol_b,
    update_b,
    own_b,
    schur_sum,
    part,
    pair_land,
    reduced,
    landing,
    message,
    gathered,
    total,
    out_send,
    out_land,
    load_sem,
    swap_send,
    swap_recv,
    halo_send,
    halo_recv,
    pair_send,
    pair_recv,
    send_b,
    recv_b,
    send_c,
    recv_c,
):
    me = lax.axis_index("ord")
    core = lax.axis_index("rhs")
    other = 1 - core
    first = core == 0
    slots, row_total, half = rhs_own.shape
    columns = 2 * half
    border_rows = resid_b.shape[0]
    rows = border_rows // count
    own_slots = pl.ds(core * slots, slots)
    other_slots = pl.ds(other * slots, slots)

    loads = [
        pltpu.make_async_copy(source.at[own_slots], target, load_sem.at[at])
        for at, (source, target) in enumerate(
            (
                (start_hbm, start_own),
                (coupling_hbm, coupling),
                (border_hbm, border),
                (diag_hbm, diag),
                (rhs_hbm, rhs_own),
                (inverse_hbm, inverse),
            )
        )
    ]
    for load in loads:
        load.start()

    def peer(step):
        return lax.rem(me + step, count)

    def source(step):
        return lax.rem(me + count - step, count)

    sibling = (me, other)
    beyond = (lax.rem(me + count + jnp.where(first, -1, 1), count), other)
    following = (jnp.where(first, me, lax.rem(me + 1, count)), other)
    preceding = (jnp.where(first, lax.rem(me + count - 1, count), me), other)

    barrier = pltpu.get_barrier_semaphore()

    def greet(step, carry):
        pl.semaphore_signal(barrier, inc=1, device_id=(peer(step), core), device_id_type=MESH)
        return carry

    lax.fori_loop(1, count, greet, 0)
    pl.semaphore_signal(barrier, inc=1, device_id=sibling, device_id_type=MESH)
    pl.semaphore_signal(barrier, inc=1, device_id=beyond, device_id_type=MESH)
    pl.semaphore_wait(barrier, count + 1)

    def remote(source_ref, target_ref, send_sem, recv_sem, device):
        return pltpu.make_async_remote_copy(
            src_ref=source_ref,
            dst_ref=target_ref,
            send_sem=send_sem,
            recv_sem=recv_sem,
            device_id=device,
            device_id_type=MESH,
        )

    swaps = [
        remote(source_ref, target, swap_send.at[at], swap_recv.at[at], sibling)
        for at, (source_ref, target) in enumerate(
            (
                (start_hbm.at[other_slots], start_land),
                (start_border_ref, start_border_land),
                (rhs_hbm.at[other_slots], rhs_land),
                (rhs_border_ref, rhs_border_land),
            )
        )
    ]
    for swap in swaps:
        swap.start()

    def joined(own, theirs):
        return jnp.concatenate(
            [jnp.where(first, own, theirs), jnp.where(first, theirs, own)], 1
        )

    def live(slot, value):
        at_row = lax.broadcasted_iota(jnp.int32, value.shape, 0)
        return jnp.where(at_row < counts_ref[core * slots + slot], value, 0.0)

    def each_slot(body):
        def step(slot, carry):
            body(slot)
            return carry

        lax.fori_loop(0, slots, step, 0)

    def folded(value):
        return jnp.sum(value.reshape(row_total // 8, 8, columns), axis=0)

    def operate(border_narrow):
        last = slots - 1
        lower_send[...] = mm(coupling_t[last], narrow[last]).astype(BF16)
        down = remote(lower_send, lower, halo_send.at[0], halo_recv.at[0], following)
        up = remote(narrow.at[0], upper, halo_send.at[1], halo_recv.at[1], preceding)
        down.start()
        up.start()
        own_b[...] = mm(corner_ref[...], border_narrow)

        def local(slot):
            return mm(diag[slot], narrow[slot]) + mm(border[slot], border_narrow)

        def behind(slot):
            return mm(coupling_t[slot - 1], narrow[slot - 1])

        def inner(slot, carry):
            applied[slot] = local(slot) + mm(coupling[slot], narrow[slot + 1]) + behind(slot)
            return carry

        lax.fori_loop(1, last, inner, 0)
        top = local(0) + mm(coupling[0], narrow[1])
        applied[last] = local(last) + behind(last)
        down.wait_recv()
        is_first = jnp.logical_and(me == 0, first)
        applied[0] = top + jnp.where(is_first, 0.0, lower[...].astype(F32))
        up.wait_recv()
        is_last = jnp.logical_and(me == count - 1, core == 1)
        ahead = jnp.where(is_last, 0.0, upper[...].astype(F32)).astype(BF16)
        applied[last] = applied[last] + mm(coupling[last], ahead)
        down.wait_send()
        up.wait_send()

    def rows_of(device):
        return pl.ds(pl.multiple_of(device * rows, rows), rows)

    def sum_border(numerators, denominators):
        swap = remote(
            part.at[other], pair_land, pair_send.at[0], pair_recv.at[0], sibling
        )
        swap.start()
        swap.wait_recv()
        reduced[...] = part[core] + pair_land[...]

        def scatter(step):
            return remote(
                reduced.at[rows_of(peer(step))],
                landing.at[step],
                send_b.at[step],
                recv_b.at[step],
                (peer(step), core),
            )

        def scatter_start(step, carry):
            scatter(step).start()
            return carry

        def scatter_wait(step, so_far):
            scatter(step).wait_recv()
            return so_far + landing[step]

        lax.fori_loop(1, count, scatter_start, 0)
        mine = lax.fori_loop(1, count, scatter_wait, reduced[rows_of(me)])
        border_part = jnp.where(first, own_b[rows_of(me)] + mine, 0.0)
        against = resid_b[rows_of(me)] * border_part
        squares = border_part * border_part
        message[:rows] = mine
        message[rows : rows + 8] = numerators + jnp.sum(
            against.reshape(rows // 8, 8, columns), axis=0
        )
        message[rows + 8 :] = denominators + jnp.sum(
            squares.reshape(rows // 8, 8, columns), axis=0
        )

        def gather(step, slot):
            return remote(
                message,
                gathered.at[slot],
                send_c.at[step],
                recv_c.at[step],
                (peer(step), core),
            )

        def gather_start(step, carry):
            gather(step, me).start()
            return carry

        def gather_wait(step, carry):
            gather(step, source(step)).wait_recv()
            return carry

        lax.fori_loop(1, count, gather_start, 0)
        gathered[me] = message[...]
        lax.fori_loop(1, count, gather_wait, 0)

        def place(device, tiles):
            total[core, rows_of(device)] = gathered[device, :rows, :]
            return tiles + gathered[device, rows:, :]

        tiles = lax.fori_loop(0, count, place, jnp.zeros((16, columns), F32))
        total[core, border_rows:] = tiles
        back = remote(
            total.at[core], total.at[core], pair_send.at[1], pair_recv.at[1], sibling
        )
        back.start()
        landed = remote(
            total.at[other], total.at[other], pair_send.at[1], pair_recv.at[1], sibling
        )
        landed.wait_recv()
        back.wait_send()
        swap.wait_send()

        def drain(step, carry):
            scatter(step).wait_send()
            gather(step, me).wait_send()
            return carry

        lax.fori_loop(1, count, drain, 0)
        both = total[0, border_rows:] + total[1, border_rows:]
        return (jnp.sum(both[:8]), jnp.sum(both[8:]))

    zero_tile = jnp.zeros((8, columns), F32)

    loads[0].wait()
    swaps[0].wait_recv()

    def begin(slot):
        value = live(slot, joined(start_own[slot], start_land[slot]))
        sol[slot] = value
        narrow[slot] = value.astype(BF16)

    each_slot(begin)
    loads[1].wait()

    def turn_coupling(slot):
        coupling_t[slot] = coupling[slot].T

    each_slot(turn_coupling)
    loads[2].wait()

    def turn_border(slot):
        border_t[slot] = border[slot].T

    each_slot(turn_border)
    swaps[1].wait_recv()
    sol_b[...] = joined(start_border_ref[...], start_border_land[...])
    loads[3].wait()
    operate(sol_b[...].astype(BF16))
    loads[4].wait()
    loads[5].wait()
    swaps[2].wait_recv()
    swaps[3].wait_recv()
    part[...] = jnp.zeros_like(part)

    def to_border(slot, blockwise):
        pair = jnp.concatenate([narrow[slot], blockwise.astype(BF16)], 1)
        sums = mm(border_t[slot], pair)
        part[0] = part[0] + sums[:, :columns]
        part[1] = part[1] + sums[:, columns:]

    def first_residual(slot):
        value = live(slot, joined(rhs_own[slot], rhs_land[slot]) - applied[slot])
        resid[slot] = value
        to_border(slot, live(slot, mm(inverse[slot], value.astype(BF16))))

    each_slot(first_residual)
    resid_b[...] = joined(rhs_border_ref[...], rhs_border_land[...])
    sum_border(zero_tile, zero_tile)
    resid_b[...] = resid_b[...] - (own_b[...] + total[0, :border_rows])
    schur_sum[...] = total[1, :border_rows]

    step_size = None
    for iteration in range(ITERS):
        more = iteration < ITERS - 1
        update_b[...] = jnp.dot(
            schur_ref[...],
            resid_b[...] - schur_sum[...],
            precision=lax.Precision.HIGHEST,
            preferred_element_type=F32,
        )
        border_narrow = update_b[...].astype(BF16)

        def precondition(slot, step_size=step_size, border_narrow=border_narrow):
            if step_size is not None:
                sol[slot] = sol[slot] + step_size * update[slot]
                resid[slot] = resid[slot] - step_size * applied[slot]
            lifted = mm(border[slot], border_narrow).astype(BF16)
            both = mm(
                inverse[slot], jnp.concatenate([resid[slot].astype(BF16), lifted], 1)
            )
            value = live(slot, both[:, :columns] - both[:, columns:])
            update[slot] = value
            narrow[slot] = value.astype(BF16)

        each_slot(precondition)
        operate(border_narrow)
        part[...] = jnp.zeros_like(part)

        def products(slot, carry, more=more):
            numerators, denominators = carry
            value = live(slot, applied[slot])
            applied[slot] = value
            if more:
                to_border(slot, live(slot, mm(inverse[slot], value.astype(BF16))))
            else:
                part[0] = part[0] + mm(border_t[slot], narrow[slot])
            return (
                numerators + folded(resid[slot] * value),
                denominators + folded(value * value),
            )

        tiles = lax.fori_loop(0, slots, products, (zero_tile, zero_tile))
        numerator, denominator = sum_border(*tiles)
        step_size = numerator / (denominator + 1e-06)
        sol_b[...] = sol_b[...] + step_size * update_b[...]
        if more:
            applied_b = own_b[...] + total[0, :border_rows]
            resid_b[...] = resid_b[...] - step_size * applied_b
            schur_sum[...] = schur_sum[...] - step_size * total[1, :border_rows]

    def finish(slot):
        value = sol[slot] + step_size * update[slot]
        left, right = (value[:, :half], value[:, half:])
        out_ref[core * slots + slot] = jnp.where(first, left, right)
        out_send[slot] = jnp.where(first, right, left)

    each_slot(finish)
    share = remote(out_send, out_land, swap_send.at[4], swap_recv.at[4], sibling)
    share.start()
    out_border_ref[...] = jnp.where(first, sol_b[:, :half], sol_b[:, half:])
    for swap in swaps:
        swap.wait_send()
    share.wait_recv()

    def place_out(slot):
        out_ref[other * slots + slot] = out_land[slot]

    each_slot(place_out)
    share.wait_send()


def shards(
    rhs_blocks,
    rhs_border,
    start_blocks,
    start_border,
    diag_blocks,
    block_inverses,
    couplings,
    border_couplings,
    border_block,
    schur_inverse,
    row_counts,
):
    count = lax.axis_size("ord")
    slots = rhs_blocks.shape[0] // 2
    row_total, half = rhs_blocks.shape[1:]
    columns = 2 * half
    border_rows = rhs_border.shape[0]
    rows = border_rows // count
    vmem = pl.BlockSpec(memory_space=pltpu.VMEM)
    anywhere = pl.BlockSpec(memory_space=pl.ANY)
    square = pltpu.VMEM((slots, row_total, row_total), BF16)
    halves = pltpu.VMEM((slots, row_total, half), F32)
    border_half = pltpu.VMEM((border_rows, half), F32)
    state = pltpu.VMEM((slots, row_total, columns), F32)
    edge = pltpu.VMEM((row_total, columns), BF16)
    border_state = pltpu.VMEM((border_rows, columns), F32)
    sems = pltpu.SemaphoreType.DMA
    return pl.pallas_call(
        functools.partial(kernel, count),
        out_shape=(
            jax.ShapeDtypeStruct(rhs_blocks.shape, F32),
            jax.ShapeDtypeStruct(rhs_border.shape, F32),
        ),
        in_specs=[anywhere] * 6 + [vmem] * 4 + [pl.BlockSpec(memory_space=pltpu.SMEM)],
        out_specs=(vmem, vmem),
        scratch_shapes=[
            square,
            square,
            square,
            square,
            pltpu.VMEM((slots, row_total, border_rows), BF16),
            pltpu.VMEM((slots, border_rows, row_total), BF16),
            halves,
            halves,
            halves,
            halves,
            border_half,
            border_half,
            state,
            state,
            state,
            state,
            pltpu.VMEM((slots, row_total, columns), BF16),
            edge,
            edge,
            edge,
            border_state,
            border_state,
            border_state,
            border_state,
            border_state,
            pltpu.VMEM((2, border_rows, columns), F32),
            border_state,
            border_state,
            pltpu.VMEM((count, rows, columns), F32),
            pltpu.VMEM((rows + 16, columns), F32),
            pltpu.VMEM((count, rows + 16, columns), F32),
            pltpu.VMEM((2, border_rows + 16, columns), F32),
            halves,
            halves,
            sems((6,)),
            sems((5,)),
            sems((5,)),
            sems((2,)),
            sems((2,)),
            sems((2,)),
            sems((2,)),
            sems((count,)),
            sems((count,)),
            sems((count,)),
            sems((count,)),
        ],
        compiler_params=pltpu.CompilerParams(
            collective_id=0, has_side_effects=True, vmem_limit_bytes=58 * 2**20
        ),
        name="minimal_residual",
    )(
        rhs_blocks,
        start_blocks,
        diag_blocks,
        block_inverses,
        couplings,
        border_couplings,
        rhs_border,
        start_border,
        border_block,
        schur_inverse,
        row_counts,
    )


def solution(mesh):
    return jax.shard_map(
        shards,
        mesh=mesh,
        in_specs=(
            P("ord", None, "rhs"),
            P(None, "rhs"),
            P("ord", None, "rhs"),
            P(None, "rhs"),
            P("ord", None, None),
            P("ord", None, None),
            P("ord", None, None),
            P("ord", None, None),
            P(),
            P(),
            P("ord"),
        ),
        out_specs=(P("ord", None, "rhs"), P(None, "rhs")),
        check_vma=False,
    )
```

time: 816 us -> 168 us (0.21)
  waiting for transfers between devices: 487 us -> 0 us
  Pallas kernels: 0 us -> 154 us
  blocking collectives: 128 us -> 0 us
  matrix products: 116 us -> 0 us
  between operations: 26.6 us -> 0.66 us
  starting transfers between devices: 25.6 us -> 0 us
  other arithmetic: 10.4 us -> 0 us
  local copies, waits for them, and re-layouts: 21.4 us -> 12.4 us
    psum x6 -> x0, waiting for transfers between devices: 487 us -> none  [the longest x4 281 us: operate(): lax.psum((gathered, block_numerator, block_denominator), 'ord')]
    pallas_call x0 -> x1, Pallas kernels: none -> 154 us  [shards(): pl.pallas_call(functools.partial(kernel, count), out_shape=(jax.ShapeDtyp...]
    psum x6 -> x0, blocking collectives: 128 us -> none  [the longest x3 119 us: operate(): lax.psum((gathered, block_numerator, block_denominator), 'ord')]
    dot_general x36 -> x0, matrix products: 116 us -> none  [the longest x14 64.4 us: batched(): jnp.einsum('sij,sjc->sic', matrices, vectors, preferred_element_type=jnp....]
    ppermute x8 -> x0, starting transfers between devices: 24.7 us -> none  [shifted(): lax.ppermute(value, axis, [(source, source + steps) for source in range(l...]
    slice x16 -> x0, local copies, waits for them, and re-layouts: 14 us -> none  [the longest x4 7.44 us: operate(): behind = jnp.concatenate([lower, transposed[:-1]], 0)]
  transfers between devices with their start and end apart: 14 -> 0, of which waited for: 6 -> 0; matrix products, arithmetic and copies ran while one was open for 6% -> 0% of each run, Pallas kernels for 0% -> 0%
where the time goes in v1:
time: 168 us; the launch traced here: 167 us
  Pallas kernels  154 us (92%)
  local copies, waits for them, and re-layouts  12.4 us (7%)
    pallas_call x1, Pallas kernels, shards(): pl.pallas_call(functools.partial(kernel, count), out_shape=(jax.ShapeDtyp...  154 us
    unnamed x8, local copies, waits for them, and re-layouts  8.62 us
    pallas_call x2, local copies, waits for them, and re-layouts, shards(): pl.pallas_call(functools.partial(kernel, count), out_shape=(jax.ShapeDtyp...  3.76 us

profile of v1, /device:TPU:0, one launch (start us, length us, event | category | flops | bytes accessed | tf_op | source)
XLA Modules:
  0.0 166.7 jit_solution(1095532668178916153)
XLA Ops:
  0.6 0.0 copy-start
  0.6 1.8 %copy.15.rhs_border_ref = f32[512,64]{1,0:T(8,128)} copy(f32[512,64]{0,1:T(8,128)} %param.12) | data formatting | bytes 262144 | tf_op args[1]
  2.5 1.7 %copy.16.start_border_ref = f32[512,64]{1,0:T(8,128)} copy(f32[512,64]{0,1:T(8,128)} %param.14) | data formatting | bytes 262144 | tf_op args[3]
  4.2 3.0 %copy.13.rhs_hbm = f32[8,640,64]{2,1,0:T(8,128)} copy(f32[8,640,64]{1,2,0:T(8,128)} %param.11) | data formatting | bytes 2621440 | tf_op args[0]
  7.2 0.0 copy-done
  7.2 2.0 %copy.14.start_hbm = f32[8,640,64]{2,1,0:T(8,128)} copy(f32[8,640,64]{1,2,0:T(8,128)S(1)} %copy-done) | data formatting | bytes 2621440 | tf_op args[2]
  9.3 153.7 %minimal_residual.1 = (f32[8,640,64]{2,1,0:T(8,128)}, f32[512,64]{1,0:T(8,128)}) custom-call(f32[8,640,64]{2,1,0:T(8,128)} %copy.13.rhs_hbm, f32[8,640,64]{2,1,0:T(8,128)} %copy.14.start_hbm, bf16[8,640,640]{2,1,0:T(8,128)(2,1)} %diag_hbm.1, bf16[8,640,640]{2,1,0:T(8,128)(2,1)} %inverse_hbm.1, bf16[8,640,640]{2,1,0:T(8,128)(2,1)} %coupling_hbm.1, ...), custom_call_target="tpu_custom_call" | custom-call | tf_op jit(solution)/shard_map/minimal_residual/pallas_call | solution.py:441
  162.9 0.0 copy-start.1
  163.0 3.0 %copy.17 = f32[8,640,64]{1,2,0:T(8,128)} copy(f32[8,640,64]{2,1,0:T(8,128)} %get-tuple-element.2) | data formatting | bytes 2621440 | tf_op jit(solution)/shard_map/minimal_residual/pallas_call | solution.py:441
  165.9 0.0 copy-done.1
  165.9 0.8 copy.18
Async XLA Ops:
  0.6 6.6 %copy-start = (f32[8,640,64]{1,2,0:T(8,128)S(1)}, f32[8,640,64]{1,2,0:T(8,128)}, u32[]{:S(2)}) copy-start(f32[8,640,64]{1,2,0:T(8,128)} %param.13) | copy-start | bytes 3932164
  162.9 3.0 %copy-start.1 = (f32[512,64]{1,0:T(8,128)S(1)}, f32[512,64]{1,0:T(8,128)}, u32[]{:S(2)}) copy-start(f32[512,64]{1,0:T(8,128)} %get-tuple-element.3) | copy-start | bytes 393220

commit v2 on v1

--- a/solution.py
+++ b/solution.py
@@ -63,6 +63,7 @@
     landing,
     message,
     gathered,
+    last_tiles,
     total,
     out_send,
     out_land,
@@ -77,12 +78,13 @@
     recv_b,
     send_c,
     recv_c,
+    recv_last,
 ):
     me = lax.axis_index("ord")
     core = lax.axis_index("rhs")
     other = 1 - core
     first = core == 0
-    slots, row_total, half = rhs_own.shape
+    slots, half, row_total = rhs_own.shape
     columns = 2 * half
     border_rows = resid_b.shape[0]
     rows = border_rows // count
@@ -106,10 +108,12 @@
         load.start()
 
     def peer(step):
-        return lax.rem(me + step, count)
+        ahead = me + step
+        return jnp.where(ahead >= count, ahead - count, ahead)
 
     def source(step):
-        return lax.rem(me + count - step, count)
+        behind = me - step
+        return jnp.where(behind < 0, behind + count, behind)
 
     sibling = (me, other)
     beyond = (lax.rem(me + count + jnp.where(first, -1, 1), count), other)
@@ -153,8 +157,8 @@
 
     def joined(own, theirs):
         return jnp.concatenate(
-            [jnp.where(first, own, theirs), jnp.where(first, theirs, own)], 1
-        )
+            [jnp.where(first, own, theirs), jnp.where(first, theirs, own)], 0
+        ).T
 
     def live(slot, value):
         at_row = lax.broadcasted_iota(jnp.int32, value.shape, 0)
@@ -205,7 +209,7 @@
     def rows_of(device):
         return pl.ds(pl.multiple_of(device * rows, rows), rows)
 
-    def sum_border(numerators, denominators):
+    def sum_border(numerators, denominators, final=False):
         swap = remote(
             part.at[other], pair_land, pair_send.at[0], pair_recv.at[0], sibling
         )
@@ -230,25 +234,37 @@
             scatter(step).wait_recv()
             return so_far + landing[step]
 
-        lax.fori_loop(1, count, scatter_start, 0)
-        mine = lax.fori_loop(1, count, scatter_wait, reduced[rows_of(me)])
+        def scatter_drain(step, carry):
+            scatter(step).wait_send()
+            return carry
+
+        def reduce_rows():
+            lax.fori_loop(1, count, scatter_start, 0)
+            message[:rows] = lax.fori_loop(1, count, scatter_wait, reduced[rows_of(me)])
+
+        if final:
+            pl.when(first)(reduce_rows)
+        else:
+            reduce_rows()
+        mine = message[:rows]
         border_part = jnp.where(first, own_b[rows_of(me)] + mine, 0.0)
         against = resid_b[rows_of(me)] * border_part
         squares = border_part * border_part
-        message[:rows] = mine
-        message[rows : rows + 8] = numerators + jnp.sum(
-            against.reshape(rows // 8, 8, columns), axis=0
-        )
-        message[rows + 8 :] = denominators + jnp.sum(
-            squares.reshape(rows // 8, 8, columns), axis=0
+        numerators = numerators + jnp.sum(against.reshape(rows // 8, 8, columns), axis=0)
+        denominators = denominators + jnp.sum(squares.reshape(rows // 8, 8, columns), axis=0)
+        tile_row = lax.broadcasted_iota(jnp.int32, (8, columns), 0)
+        message[rows:] = jnp.where(
+            tile_row == 0,
+            jnp.sum(numerators, axis=0, keepdims=True),
+            jnp.where(tile_row == 1, jnp.sum(denominators, axis=0, keepdims=True), 0.0),
         )
 
         def gather(step, slot):
             return remote(
-                message,
-                gathered.at[slot],
+                message.at[pl.ds(rows, 8)] if final else message,
+                last_tiles.at[slot] if final else gathered.at[slot],
                 send_c.at[step],
-                recv_c.at[step],
+                recv_last.at[step] if final else recv_c.at[step],
                 (peer(step), core),
             )
 
@@ -261,34 +277,46 @@
             return carry
 
         lax.fori_loop(1, count, gather_start, 0)
-        gathered[me] = message[...]
+        if final:
+            last_tiles[me] = message[rows:]
+        else:
+            gathered[me] = message[...]
         lax.fori_loop(1, count, gather_wait, 0)
 
         def place(device, tiles):
+            if final:
+                return tiles + last_tiles[device]
             total[core, rows_of(device)] = gathered[device, :rows, :]
             return tiles + gathered[device, rows:, :]
 
-        tiles = lax.fori_loop(0, count, place, jnp.zeros((16, columns), F32))
+        tiles = lax.fori_loop(0, count, place, jnp.zeros((8, columns), F32))
         total[core, border_rows:] = tiles
-        back = remote(
-            total.at[core], total.at[core], pair_send.at[1], pair_recv.at[1], sibling
-        )
+
+        def half_total(owner):
+            ref = total.at[owner, pl.ds(border_rows, 8)] if final else total.at[owner]
+            return remote(ref, ref, pair_send.at[1], pair_recv.at[1], sibling)
+
+        back = half_total(core)
         back.start()
-        landed = remote(
-            total.at[other], total.at[other], pair_send.at[1], pair_recv.at[1], sibling
-        )
+        landed = half_total(other)
         landed.wait_recv()
         back.wait_send()
         swap.wait_send()
 
         def drain(step, carry):
-            scatter(step).wait_send()
             gather(step, me).wait_send()
             return carry
 
+        def drain_rows():
+            lax.fori_loop(1, count, scatter_drain, 0)
+
+        if final:
+            pl.when(first)(drain_rows)
+        else:
+            drain_rows()
         lax.fori_loop(1, count, drain, 0)
         both = total[0, border_rows:] + total[1, border_rows:]
-        return (jnp.sum(both[:8]), jnp.sum(both[8:]))
+        return (jnp.sum(both[0:1]), jnp.sum(both[1:2]))
 
     zero_tile = jnp.zeros((8, columns), F32)
 
@@ -381,7 +409,7 @@
             )
 
         tiles = lax.fori_loop(0, slots, products, (zero_tile, zero_tile))
-        numerator, denominator = sum_border(*tiles)
+        numerator, denominator = sum_border(*tiles, final=not more)
         step_size = numerator / (denominator + 1e-06)
         sol_b[...] = sol_b[...] + step_size * update_b[...]
         if more:
@@ -391,14 +419,16 @@
 
     def finish(slot):
         value = sol[slot] + step_size * update[slot]
-        left, right = (value[:, :half], value[:, half:])
+        turned = value.T
+        left, right = (turned[:half], turned[half:])
         out_ref[core * slots + slot] = jnp.where(first, left, right)
         out_send[slot] = jnp.where(first, right, left)
 
     each_slot(finish)
     share = remote(out_send, out_land, swap_send.at[4], swap_recv.at[4], sibling)
     share.start()
-    out_border_ref[...] = jnp.where(first, sol_b[:, :half], sol_b[:, half:])
+    turned_b = sol_b[...].T
+    out_border_ref[...] = jnp.where(first, turned_b[:half], turned_b[half:])
     for swap in swaps:
         swap.wait_send()
     share.wait_recv()
@@ -432,17 +462,17 @@
     vmem = pl.BlockSpec(memory_space=pltpu.VMEM)
     anywhere = pl.BlockSpec(memory_space=pl.ANY)
     square = pltpu.VMEM((slots, row_total, row_total), BF16)
-    halves = pltpu.VMEM((slots, row_total, half), F32)
-    border_half = pltpu.VMEM((border_rows, half), F32)
+    halves = pltpu.VMEM((slots, half, row_total), F32)
+    border_half = pltpu.VMEM((half, border_rows), F32)
     state = pltpu.VMEM((slots, row_total, columns), F32)
     edge = pltpu.VMEM((row_total, columns), BF16)
     border_state = pltpu.VMEM((border_rows, columns), F32)
     sems = pltpu.SemaphoreType.DMA
-    return pl.pallas_call(
+    turned_blocks, turned_border = pl.pallas_call(
         functools.partial(kernel, count),
         out_shape=(
-            jax.ShapeDtypeStruct(rhs_blocks.shape, F32),
-            jax.ShapeDtypeStruct(rhs_border.shape, F32),
+            jax.ShapeDtypeStruct((2 * slots, half, row_total), F32),
+            jax.ShapeDtypeStruct((half, border_rows), F32),
         ),
         in_specs=[anywhere] * 6 + [vmem] * 4 + [pl.BlockSpec(memory_space=pltpu.SMEM)],
         out_specs=(vmem, vmem),
@@ -476,9 +506,10 @@
             border_state,
             border_state,
             pltpu.VMEM((count, rows, columns), F32),
-            pltpu.VMEM((rows + 16, columns), F32),
-            pltpu.VMEM((count, rows + 16, columns), F32),
-            pltpu.VMEM((2, border_rows + 16, columns), F32),
+            pltpu.VMEM((rows + 8, columns), F32),
+            pltpu.VMEM((count, rows + 8, columns), F32),
+            pltpu.VMEM((count, 8, columns), F32),
+            pltpu.VMEM((2, border_rows + 8, columns), F32),
             halves,
             halves,
             sems((6,)),
@@ -492,24 +523,26 @@
             sems((count,)),
             sems((count,)),
             sems((count,)),
+            sems((count,)),
         ],
         compiler_params=pltpu.CompilerParams(
             collective_id=0, has_side_effects=True, vmem_limit_bytes=58 * 2**20
         ),
         name="minimal_residual",
     )(
-        rhs_blocks,
-        start_blocks,
+        jnp.swapaxes(rhs_blocks, 1, 2),
+        jnp.swapaxes(start_blocks, 1, 2),
         diag_blocks,
         block_inverses,
         couplings,
         border_couplings,
-        rhs_border,
-        start_border,
+        rhs_border.T,
+        start_border.T,
         border_block,
         schur_inverse,
         row_counts,
     )
+    return (jnp.swapaxes(turned_blocks, 1, 2), turned_border.T)
 
 
 def solution(mesh):

time: 168 us -> 148 us (0.88)
  Pallas kernels: 154 us -> 143 us
  local copies, waits for them, and re-layouts: 12.4 us -> 4.04 us
    pallas_call x1, Pallas kernels: 154 us -> 143 us  [shards(): pl.pallas_call(functools.partial(kernel, count), out_shape=(jax.ShapeDtyp...]
    unnamed x8 -> x2, local copies, waits for them, and re-layouts: 8.62 us -> 4.04 us
    pallas_call x2 -> x0, local copies, waits for them, and re-layouts: 3.76 us -> none  [shards(): pl.pallas_call(functools.partial(kernel, count), out_shape=(jax.ShapeDtyp...]
where the time goes in v2:
time: 148 us; the launch traced here: 147 us
  Pallas kernels  143 us (97%)
  local copies, waits for them, and re-layouts  4.04 us (3%)
    pallas_call x1, Pallas kernels, shards(): pl.pallas_call(functools.partial(kernel, count), out_shape=(jax.ShapeDtyp...  143 us
    unnamed x2, local copies, waits for them, and re-layouts  4.04 us

profile of v2, /device:TPU:0, one launch (start us, length us, event | category | flops | bytes accessed | tf_op | source)
XLA Modules:
  0.0 147.4 jit_solution(9474149773527239139)
XLA Ops:
  0.6 142.7 %minimal_residual.1 = (f32[8,64,640]{2,1,0:T(8,128)}, f32[64,512]{1,0:T(8,128)}) custom-call(f32[8,64,640]{2,1,0:T(8,128)} %bitcast.7, f32[8,64,640]{2,1,0:T(8,128)} %bitcast.8, bf16[8,640,640]{2,1,0:T(8,128)(2,1)} %diag_hbm.1, bf16[8,640,640]{2,1,0:T(8,128)(2,1)} %inverse_hbm.1, bf16[8,640,640]{2,1,0:T(8,128)(2,1)} %coupling_hbm.1, ...), custom_call_target="tpu_custom_call" | custom-call | tf_op jit(solution)/shard_map/minimal_residual/pallas_call | solution.py:471
  143.4 2.5 %copy.15 = f32[8,640,64]{1,2,0:T(8,128)} copy(f32[8,640,64]{1,2,0:T(8,128)} %bitcast.6) | data formatting | bytes 2621440
  145.8 1.6 %copy.16 = f32[512,64]{0,1:T(8,128)} copy(f32[512,64]{0,1:T(8,128)} %bitcast.11) | data formatting | bytes 262144

commit v3 on v2

--- a/solution.py
+++ b/solution.py
@@ -408,7 +408,7 @@
                 denominators + folded(value * value),
             )
 
-        tiles = lax.fori_loop(0, slots, products, (zero_tile, zero_tile))
+        tiles = lax.fori_loop(0, slots, products, (zero_tile, zero_tile), unroll=True)
         numerator, denominator = sum_border(*tiles, final=not more)
         step_size = numerator / (denominator + 1e-06)
         sol_b[...] = sol_b[...] + step_size * update_b[...]

time: 148 us -> 146 us (0.986)
  no operation moved by 1% of the time
where the time goes in v3:
time: 146 us
  Pallas kernels  142 us (97%)
  local copies, waits for them, and re-layouts  4.04 us (3%)
    pallas_call x1, Pallas kernels, shards(): pl.pallas_call(functools.partial(kernel, count), out_shape=(jax.ShapeDtyp...  142 us
    unnamed x2, local copies, waits for them, and re-layouts  4.04 us

profile of v3, /device:TPU:0, one launch (start us, length us, event | category | flops | bytes accessed | tf_op | source)
XLA Modules:
  0.0 146.3 jit_solution(4065445151068386807)
XLA Ops:
  0.6 141.6 %minimal_residual.1 = (f32[8,64,640]{2,1,0:T(8,128)}, f32[64,512]{1,0:T(8,128)}) custom-call(f32[8,64,640]{2,1,0:T(8,128)} %bitcast.7, f32[8,64,640]{2,1,0:T(8,128)} %bitcast.8, bf16[8,640,640]{2,1,0:T(8,128)(2,1)} %diag_hbm.1, bf16[8,640,640]{2,1,0:T(8,128)(2,1)} %inverse_hbm.1, bf16[8,640,640]{2,1,0:T(8,128)(2,1)} %coupling_hbm.1, ...), custom_call_target="tpu_custom_call" | custom-call | tf_op jit(solution)/shard_map/minimal_residual/pallas_call | solution.py:471
  142.2 2.5 %copy.15 = f32[8,640,64]{1,2,0:T(8,128)} copy(f32[8,640,64]{1,2,0:T(8,128)} %bitcast.6) | data formatting | bytes 2621440
  144.7 1.6 %copy.16 = f32[512,64]{0,1:T(8,128)} copy(f32[512,64]{0,1:T(8,128)} %bitcast.11) | data formatting | bytes 262144
